TPU v7x, 256 devices: a whole 4x4x8 slice. The times are simulated.
256 devices in a mesh: expert: 64 (over x, z, core), chan: 4 (over y).
Axes of the slice: x: 4, y: 4, z: 8, core: 2. Of those that a mesh axis runs over, the one named last changes fastest.
Arguments:
- rows_in: bfloat16 [2048, 6144], P('expert', 'chan'), may hold values from -6 to 6
- expert_picks: int32 [2048, 2], P('expert'), may hold values from 0 to 3, all different within a row; in each aligned block of 32 rows (0 to 31, 32 to 63, ...) at most 18 rows name the same one
- latent_ids: int32 [2048, 2, 32], P('expert'), may hold values from 0 to 8191, as said below
- enc_weight: bfloat16 [6144, 32768], P('chan', 'expert'), may hold values from -0.078125 to 0.078125
- dec_weight: bfloat16 [32768, 6144], P('expert', 'chan'), may hold values from -0.375 to 0.375
Outputs:
- recon_error: bfloat16 [2048, 6144], P('expert', 'chan')
- enc_grad: float32 [6144, 32768], P('chan', 'expert')
- dec_grad: float32 [32768, 6144], P('expert', 'chan')
Inputs may be any that keep to these rules, and one draw needn't show every extreme that they name: `expert_picks`: A row's two experts differ; among the 32 rows of one device at most 18 name one expert. latent_ids[r, j, k] lies in k * 256 to (k + 1) * 256 - 1 and numbers a latent of expert expert_picks[r, j].
All inputs are finite; a program needn't handle non-finite values.
Results may differ from a plain program's by a relative error of at most 0.0095.
Values may be sent and summed in bfloat16 or wider, within the bound.
A program may use at most 128 MiB of HBM per device.

v0:
```python
import functools

import jax
import jax.numpy as jnp
from jax import lax
from jax.experimental import pallas as pl
from jax.experimental.pallas import tpu as pltpu
from jax.sharding import PartitionSpec as P

EXPERTS = 4
TOPK = 32
CAP = 18

STRIDE = 256
BLK = 4
META = 128
PAD = 256
MESH = pl.DeviceIdType.MESH
F32, BF16 = jnp.float32, jnp.bfloat16


def nt(a, b):
    return lax.dot_general(a, b, (((1,), (1,)), ((), ())), preferred_element_type=F32)


def nn(a, b):
    return jnp.dot(a, b, preferred_element_type=F32)


def step_kernel(
    X, Y, Z, SLOTS, TOPK,
    rows_hbm, picks_hbm, ids_hbm, enc_ref, dec_ref,
    err_ref, genc_ref, gdec_ref,
    rows_ref, picks_ref, ids_ref, meta_ref, xmeta, xbuf, rh, ro, eh, eo, rowst, est, enct, dech, eye, pm, pmt, offs_out, offs,
    va, vg, vact, vpre, part, sbuf, rbuf, fin, xsend, xret, xerr,
    local_sem, q_send, q_recv, w_send, w_recv, x_send, x_recv, m_send, m_recv, va_send, va_recv,
    vg_send, vg_recv, a_send, a_recv, b_send, b_recv, s_send, s_recv,
    r_send, r_recv, e_send, e_recv, d_send, d_recv, f_send, f_recv,
):
    p, y = lax.axis_index("expert"), lax.axis_index("chan")
    h, z, x = lax.rem(p, 2), lax.rem(p // 2, Z), p // (2 * Z)
    b, v = x * 2 + h, y * 2 + h
    nb, nv = 2 * X, 2 * Y
    rd, width = rows_ref.shape
    half, lat = width // 2, enc_ref.shape[1]
    piece, mid = half // 2, Z // 2

    def at(x_, z_, h_, y_):
        return ((x_ * Z + z_) * 2 + h_, y_)

    twin = at(x, z, 1 - h, y)

    def remote(src, dst, send, recv, to):
        return pltpu.make_async_remote_copy(
            src_ref=src, dst_ref=dst, send_sem=send, recv_sem=recv, device_id=to, device_id_type=MESH
        )

    def lanes(k):
        return pl.ds(pl.multiple_of(k * half, 128), half)

    def block(k):
        return pl.ds(pl.multiple_of(k * rd, rd), rd)

    def chunk_of(s, j):
        return lax.rem(z + (2 * j - 1) * s + Z, Z)

    small_in = [
        pltpu.make_async_copy(src, dst, local_sem.at[3 + n])
        for n, (src, dst) in enumerate(((rows_hbm, rows_ref), (picks_hbm, picks_ref), (ids_hbm, ids_ref)))
    ]
    for c in small_in:
        c.start()

    barrier = pltpu.get_barrier_semaphore()
    for i in range(1, nb):
        t = lax.rem(b + i, nb)
        pl.semaphore_signal(barrier, inc=1, device_id=at(t // 2, z, lax.rem(t, 2), y), device_id_type=MESH)
    for i in range(1, Z):
        pl.semaphore_signal(barrier, inc=1, device_id=at(x, lax.rem(z + i, Z), h, y), device_id_type=MESH)
    for i in range(1, Y):
        for k in range(2):
            pl.semaphore_signal(barrier, inc=1, device_id=at(x, z, k, lax.rem(y + i, Y)), device_id_type=MESH)
    down = lax.broadcasted_iota(jnp.int32, (PAD, PAD), 0)
    across = lax.broadcasted_iota(jnp.int32, (PAD, PAD), 1)
    eye[...] = jnp.where(down == across, 1.0, 0.0).astype(BF16)
    for buf in (rh, ro, eh, eo):
        buf[:, SLOTS:, :] = jnp.zeros((Z, PAD - SLOTS, half), BF16)
    fin[SLOTS:, :] = jnp.zeros((PAD - SLOTS, half), BF16)
    for s in range(mid + 1):
        va[s, v] = jnp.zeros((8, PAD), F32)
        vg[s, v] = jnp.zeros((8, PAD), F32)
    genc_ref[...] = jnp.zeros_like(genc_ref)
    gdec_ref[...] = jnp.zeros_like(gdec_ref)

    for c in small_in:
        c.wait()
    starts = lax.broadcasted_iota(jnp.int32, (rd, TOPK), 1) * STRIDE
    first = lax.broadcasted_iota(jnp.int32, (16, rd), 0) == 0
    picked = jnp.where(first, picks_ref[0:1, :], picks_ref[1:2, :]).astype(F32).astype(BF16)
    small = lax.broadcasted_iota(jnp.int32, (rd, rd), 0) == lax.broadcasted_iota(jnp.int32, (rd, rd), 1)
    pick_columns = nt(jnp.where(small, 1.0, 0.0).astype(BF16), picked)
    meta_ref[...] = jnp.concatenate(
        [(ids_ref[:, k, :] - starts).astype(F32) for k in range(2)]
        + [pick_columns, jnp.zeros((rd, META - 2 * TOPK - 16), F32)],
        axis=1,
    ).astype(BF16)
    xmeta[block(b), :] = meta_ref[...]
    xbuf[block(b), :] = rows_ref[:, lanes(h)]
    pl.semaphore_wait(barrier, nb - 1 + Z - 1 + 2 * (Y - 1))

    def part_lanes(k, q):
        return pl.ds(pl.multiple_of(k * half + q * piece, 128), piece)

    def near(i):
        t = lax.rem(b + i, nb)
        return lax.rem(t, 2), at(t // 2, z, lax.rem(t, 2), y)

    def route_copy(i):
        _, to = near(i)
        return remote(meta_ref, xmeta.at[block(b)], q_send.at[i], q_recv.at[i], to)

    def x_copy(i, q):
        k, to = near(i)
        return remote(
            rows_ref.at[:, part_lanes(k, q)], xbuf.at[block(b), pl.ds(q * piece, piece)],
            x_send.at[i, q], x_recv.at[i, q], to,
        )

    mine = pl.ds(pl.multiple_of(h * lat, lat), lat)
    own = [
        pltpu.make_async_copy(enc_ref.at[lanes(h), :], est.at[h], local_sem.at[0]),
        pltpu.make_async_copy(dec_ref.at[:, lanes(h)], dech.at[mine], local_sem.at[1]),
    ]
    weights = [
        remote(enc_ref.at[lanes(1 - h), :], est.at[h], w_send.at[0], w_recv.at[0], twin),
        remote(dec_ref.at[:, lanes(1 - h)], dech.at[mine], w_send.at[1], w_recv.at[1], twin),
    ]
    for i in range(1, nb):
        route_copy(i).start()
    for q in range(2):
        for i in range(1, nb):
            x_copy(i, q).start()
    for c in own + weights:
        c.start()

    def turn_encoder(k):
        for i in range(lat // STRIDE):
            low = pl.multiple_of(k * lat + i * STRIDE, STRIDE)
            enct[pl.ds(low, STRIDE), :] = nt(
                eye[...], est[k, :, i * STRIDE : (i + 1) * STRIDE]
            ).astype(BF16)

    for i in range(1, nb):
        route_copy(i).wait_recv()
    nr = xbuf.shape[0]
    meta_t = nt(eye[0:META, 0:META], xmeta[...])
    xf = x.astype(F32)
    hit0 = meta_t[2 * TOPK : 2 * TOPK + 1] == xf
    hit1 = meta_t[2 * TOPK + 1 : 2 * TOPK + 2] == xf
    hit = jnp.where(hit0, 1.0, jnp.where(hit1, 1.0, 0.0))
    offe = jnp.where(hit0, meta_t[0:TOPK], jnp.where(hit1, meta_t[TOPK : 2 * TOPK], 0.0)).astype(BF16)
    before = jnp.where(down[0:nr, 0:nr] < across[0:nr, 0:nr], 1.0, 0.0).astype(BF16)
    rank = nn(jnp.broadcast_to(hit, (16, nr)).astype(BF16), before)[0:1]
    slot = jnp.where(hit > 0.5, rank, -1.0).astype(jnp.int32)
    pm[...] = jnp.where(down[:, 0:nr] == slot, 1.0, 0.0).astype(BF16)
    offs_t = nt(offe, pm[...])
    for k in range(Z):
        mine = offs_t[k * BLK : (k + 1) * BLK]
        offs_out[k] = jnp.concatenate([mine, mine], axis=0)

    def meta_copy(i):
        t = lax.rem(z + i, Z)
        return remote(offs_out.at[t], offs.at[z], m_send.at[i], m_recv.at[i], at(x, t, h, y))

    for i in range(1, Z):
        meta_copy(i).start()
    offs[z] = offs_out[z]
    own[0].wait()
    turn_encoder(h)

    def ring_copy(buf, send, recv, s, j, q):
        c = chunk_of(s, j)
        view = buf.at[c, pl.ds(0, SLOTS), pl.ds(q * piece, piece)]
        to = at(x, lax.rem(z + (1 - 2 * j) + Z, Z), h, y)
        return remote(view, view, send.at[j, s, q], recv.at[j, s, q], to)

    def ring_wait(buf, send, recv, s, j, q):
        c = chunk_of(s, j)
        view = buf.at[c, pl.ds(0, SLOTS), pl.ds(q * piece, piece)]
        remote(view, view, send.at[j, s - 1, q], recv.at[j, s - 1, q], twin).wait_recv()

    def twin_copy(src, dst, send, recv, s, j):
        c = chunk_of(s, j)
        return remote(src.at[c, pl.ds(0, SLOTS)], dst.at[c, pl.ds(0, SLOTS)], send.at[s, j], recv.at[s, j], twin)

    def order(swap, j, k):
        return 1 - k if swap and j == 1 else k

    def ring_pass(buf, send, recv, s, k, swap):
        for j in range(2):
            q = order(swap, j, k)
            ring_wait(buf, send, recv, s, j, q)
            if q == j:
                ring_copy(buf, send, recv, s, j, q).start()
            else:
                @pl.when(s < mid - 1)
                def _():
                    ring_copy(buf, send, recv, s, j, q).start()

    def ring_begin(buf, send, recv, k, swap):
        for j in range(2):
            ring_copy(buf, send, recv, 0, j, order(swap, j, k)).start()

    def ring_end(buf, send, recv):
        for j in range(2):
            ring_wait(buf, send, recv, mid, j, j)

    def ring_sent(buf, send, recv):
        for s in range(mid):
            for j in range(2):
                for q in range(2):
                    if s < mid - 1 or q == j:
                        ring_copy(buf, send, recv, s, j, q).wait_send()

    def sides(s):
        return (0,) if isinstance(s, int) and s in (0, mid) else (0, 1)

    def value_copy(buf, send, recv, s, i):
        t = lax.rem(v + i, nv)
        return remote(
            buf.at[s, v], buf.at[s, v], send.at[s, i], recv.at[s, i], at(x, z, lax.rem(t, 2), t // 2)
        )

    def value_wait(buf, send, recv, s, i):
        view = buf.at[s, lax.rem(v - i + nv, nv)]
        remote(view, view, send.at[s, i], recv.at[s, i], twin).wait_recv()

    def live_at(c, i):
        return lax.broadcasted_iota(jnp.int32, (STRIDE, PAD), 0) == offs[c, pl.ds(i, 1), :].astype(jnp.int32)

    def partial_values(buf, send, recv, weight, chunks, s):
        for j in sides(s):
            c = chunk_of(s, j)
            dense = nt(weight[...], chunks[c])
            for i in range(BLK):
                buf[s, v, j * BLK + i : j * BLK + i + 1, :] = jnp.sum(
                    jnp.where(live_at(c, i), dense[i * STRIDE : (i + 1) * STRIDE], 0.0), axis=0, keepdims=True
                )
        for i in range(1, nv):
            value_copy(buf, send, recv, s, i).start()

    def whole_values(buf, send, recv, s):
        for i in range(1, nv):
            value_wait(buf, send, recv, s, i)
        total = buf[s, 0]
        for k in range(1, nv):
            total += buf[s, k]
        return total

    def spread(values, c, i):
        return jnp.where(live_at(c, i), values, 0.0).astype(BF16)

    for q in range(2):
        for i in range(1, nb):
            x_copy(i, q).wait_recv()
        rh[z, :, q * piece : (q + 1) * piece] = nn(pm[...], xbuf[:, q * piece : (q + 1) * piece]).astype(BF16)
        ring_begin(rh, a_send, a_recv, q, False)

    def ro_copy(s, j):
        return twin_copy(rh, ro, d_send, d_recv, s, j)

    def eo_copy(s, j):
        return twin_copy(eh, eo, f_send, f_recv, s, j)

    def encode(s):
        for j in sides(s):
            ro_copy(s, j).start()
        partial_values(va, va_send, va_recv, enct, rh, s)

    def decode(s):
        values = whole_values(va, va_send, va_recv, s)
        vact[s] = values
        chunks = [chunk_of(s, j) for j in sides(s)]
        table = jnp.concatenate([values] + [offs[c] for c in chunks], axis=0).astype(BF16)
        columns = nt(eye[0:SLOTS, :], table)
        place = lax.broadcasted_iota(jnp.int32, (SLOTS, STRIDE), 1).astype(F32)
        total = None
        for i in range(BLK):
            acts = [
                jnp.where(place == columns[:, 8 + 8 * j + i : 9 + 8 * j + i], columns[:, BLK * j + i : BLK * j + i + 1], 0.0)
                for j in range(len(chunks))
            ]
            act = acts[0] if len(acts) == 1 else jnp.concatenate(acts, axis=0)
            term = nn(act.astype(BF16), dech[i * STRIDE : (i + 1) * STRIDE, :])
            total = term if total is None else total + term
        for j, c in enumerate(chunks):
            part[c] = total[j * SLOTS : (j + 1) * SLOTS]

    for c in weights:
        c.wait_recv()
    turn_encoder(1 - h)
    own[1].wait()
    encode(0)
    def encode_step(s, carry):
        ring_pass(rh, a_send, a_recv, s, 0, False)

        @pl.when(s == 2)
        def _():
            decode(0)

        @pl.when(s > 2)
        def _():
            decode(s - 2)

        ring_pass(rh, a_send, a_recv, s, 1, False)

        @pl.when(s == 1)
        def _():
            for i in range(1, Z):
                meta_copy(i).wait_recv()

        encode(s)
        return carry

    lax.fori_loop(1, mid, encode_step, 0)
    decode(mid - 2)
    ring_end(rh, a_send, a_recv)
    encode(mid)
    decode(mid - 1)

    def sum_copy(t, j, q):
        view = pl.ds(q * piece, piece)
        to = at(x, lax.rem(z + (1 - 2 * j) + Z, Z), h, y)
        return remote(
            sbuf.at[j, t - 1, :, view], rbuf.at[j, t - 1, :, view], s_send.at[j, t - 1, q], s_recv.at[j, t - 1, q], to
        )

    def transpose_rows(s):
        for j in sides(s):
            c = chunk_of(s, j)
            ro_copy(s, j).wait_recv()
            for k, src in ((h, rh), (1 - h, ro)):
                for i in range(half // 256):
                    rowst[c, pl.ds(pl.multiple_of(k * half + i * 256, 256), 256), :] = nt(
                        eye[...], src[c, :, i * 256 : (i + 1) * 256]
                    ).astype(BF16)

    def sum_step(t, k):
        for j in range(2):
            q = order(True, j, k)
            low = q * piece
            c = chunk_of(t, 1 - j)
            total = part[c, :, low : low + piece]
            if t < mid - 1 or (t < mid and q == j):
                sum_copy(t + 1, j, q).wait_recv()
                total += rbuf[j, t, :, low : low + piece].astype(F32)
            sbuf[j, t - 1, :, low : low + piece] = total.astype(BF16)
            sum_copy(t, j, q).start()

    sum_step(mid - 1, 1)
    decode(mid)
    sum_step(mid, 0)
    sum_step(mid - 1, 0)
    pmt[...] = nt(eye[0:nr, 0:nr], pm[...]).astype(BF16)
    transpose_rows(0)
    for t in range(mid - 2, 0, -1):
        sum_step(t, 1)
        transpose_rows(t)
        sum_step(t, 0)
    transpose_rows(mid - 1)
    transpose_rows(mid)

    def ret_copy(i, q):
        t = lax.rem(b + i, nb)
        return remote(
            xsend.at[block(t), pl.ds(q * piece, piece)], xret.at[x, :, part_lanes(h, q)],
            r_send.at[i, q], r_recv.at[i, q], at(t // 2, z, lax.rem(t, 2), y),
        )

    def ret_wait(i, q):
        t = lax.rem(b - i + nb, nb)
        view = xret.at[t // 2, :, part_lanes(lax.rem(t, 2), q)]
        remote(view, view, r_send.at[i, q], r_recv.at[i, q], twin).wait_recv()

    def err_copy(i, q):
        t = lax.rem(b + i, nb)
        return remote(
            err_ref.at[:, part_lanes(lax.rem(t, 2), q)], xerr.at[block(b), pl.ds(q * piece, piece)],
            e_send.at[i, q], e_recv.at[i, q], at(t // 2, z, lax.rem(t, 2), y),
        )

    for q in range(2):
        own_lanes = slice(q * piece, (q + 1) * piece)
        for j in range(2):
            sum_copy(1, j, q).wait_recv()
        fin[0:SLOTS, own_lanes] = (
            part[z, :, own_lanes] + rbuf[0, 0, :, own_lanes].astype(F32) + rbuf[1, 0, :, own_lanes].astype(F32)
        ).astype(BF16)
        xsend[:, own_lanes] = nn(pmt[...], fin[:, own_lanes]).astype(BF16)
        for i in range(1, nb):
            ret_copy(i, q).start()
        xret[x, :, part_lanes(h, q)] = xsend[block(b), own_lanes]

    for q in range(2):
        for i in range(1, nb):
            ret_wait(i, q)
        for k in range(2):
            cols = slice(k * half + q * piece, k * half + (q + 1) * piece)
            recon = xret[0, :, cols].astype(F32)
            for e in range(1, X):
                recon += xret[e, :, cols].astype(F32)
            err_ref[:, cols] = (recon - rows_ref[:, cols].astype(F32)).astype(BF16)
        for i in range(1, nb):
            err_copy(i, q).start()
        xerr[block(b), q * piece : (q + 1) * piece] = err_ref[:, part_lanes(h, q)]

    for q in range(2):
        for i in range(1, nb):
            err_copy(i, q).wait_recv()
        eh[z, :, q * piece : (q + 1) * piece] = nn(pm[...], xerr[:, q * piece : (q + 1) * piece]).astype(BF16)
        ring_begin(eh, b_send, b_recv, q, False)

    def latent_grads(s):
        for j in sides(s):
            eo_copy(s, j).start()
        partial_values(vg, vg_send, vg_recv, dech, eh, s)

    def add_dec(s):
        for j in sides(s):
            eo_copy(s, j).wait_recv()
        nblk = lat // STRIDE
        acts = []
        for j in sides(s):
            c = chunk_of(s, j)
            blocks = [spread(vact[s, pl.ds(j * BLK + h * nblk + i, 1), :], c, h * nblk + i) for i in range(nblk)]
            acts.append((c, jnp.concatenate(blocks, axis=0)))
        for k, src in ((h, eh), (1 - h, eo)):
            gdec_ref[:, lanes(k)] += sum(nn(a, src[c]) for c, a in acts)

    def add_enc(s):
        vpre[s] = whole_values(vg, vg_send, vg_recv, s)
        for i in range(lat // STRIDE):
            blk = h * (lat // STRIDE) + i
            low = i * STRIDE
            pres = [(chunk_of(s, j), spread(vpre[s, pl.ds(j * BLK + blk, 1), :], chunk_of(s, j), blk)) for j in sides(s)]
            for k in range(2):
                cols = slice(k * half, (k + 1) * half)
                genc_ref[cols, low : low + STRIDE] += sum(nt(rowst[c, cols, :], g) for c, g in pres)

    latent_grads(0)

    def gradient_step(s, carry):
        ring_pass(eh, b_send, b_recv, s, 0, False)

        @pl.when(s == 1)
        def _():
            add_dec(0)

        @pl.when(s == 2)
        def _():
            add_enc(0)

        @pl.when(s > 2)
        def _():
            add_enc(s - 2)

        ring_pass(eh, b_send, b_recv, s, 1, False)
        latent_grads(s)

        @pl.when(s > 1)
        def _():
            add_dec(s - 1)

        return carry

    lax.fori_loop(1, mid, gradient_step, 0)
    add_enc(mid - 2)
    ring_end(eh, b_send, b_recv)
    latent_grads(mid)
    add_dec(mid - 1)
    add_enc(mid - 1)
    add_dec(mid)
    add_enc(mid)

    for i in range(1, nb):
        route_copy(i).wait_send()
        for q in range(2):
            x_copy(i, q).wait_send()
            ret_copy(i, q).wait_send()
            err_copy(i, q).wait_send()
    for c in weights:
        c.wait_send()
    for i in range(1, Z):
        meta_copy(i).wait_send()
    ring_sent(rh, a_send, a_recv)
    ring_sent(eh, b_send, b_recv)
    for t in range(mid, 0, -1):
        for j in range(2):
            for q in range(2):
                if t < mid or q == j:
                    sum_copy(t, j, q).wait_send()

    def sent(s):
        for i in range(1, nv):
            value_copy(va, va_send, va_recv, s, i).wait_send()
            value_copy(vg, vg_send, vg_recv, s, i).wait_send()
        for j in sides(s):
            ro_copy(s, j).wait_send()
            eo_copy(s, j).wait_send()

    def sent_step(s, carry):
        sent(s)
        return carry

    sent(0)
    lax.fori_loop(1, mid, sent_step, 0)
    sent(mid)


def per_device(experts, topk, cap, rows_in, expert_picks, latent_ids, enc_weight, dec_weight):
    X, Y = experts, lax.axis_size("chan")
    Z = lax.axis_size("expert") // (2 * X)
    rd, width = rows_in.shape
    lat, half, mid = enc_weight.shape[1], width // 2, Z // 2
    nb, nv = 2 * X, 2 * Y
    slots = min(-(-cap * nb // 16) * 16, PAD)
    vmem, hbm = pl.BlockSpec(memory_space=pltpu.VMEM), pl.BlockSpec(memory_space=pltpu.HBM)
    dma = pltpu.SemaphoreType.DMA
    scratch = [
        pltpu.VMEM(rows_in.shape, BF16),
        pltpu.VMEM((2, rd), jnp.int32),
        pltpu.VMEM(latent_ids.shape, jnp.int32),
        pltpu.VMEM((rd, META), BF16),
        pltpu.VMEM((nb * rd, META), BF16),
        pltpu.VMEM((nb * rd, half), BF16),
        pltpu.VMEM((Z, PAD, half), BF16),
        pltpu.VMEM((Z, PAD, half), BF16),
        pltpu.VMEM((Z, PAD, half), BF16),
        pltpu.VMEM((Z, PAD, half), BF16),
        pltpu.VMEM((Z, width, PAD), BF16),
        pltpu.VMEM((2, half, lat), BF16),
        pltpu.VMEM((2 * lat, half), BF16),
        pltpu.VMEM((2 * lat, half), BF16),
        pltpu.VMEM((PAD, PAD), BF16),
        pltpu.VMEM((PAD, nb * rd), BF16),
        pltpu.VMEM((nb * rd, PAD), BF16),
        pltpu.VMEM((Z, 8, PAD), F32),
        pltpu.VMEM((Z, 8, PAD), F32),
        pltpu.VMEM((mid + 1, nv, 8, PAD), F32),
        pltpu.VMEM((mid + 1, nv, 8, PAD), F32),
        pltpu.VMEM((mid + 1, 8, PAD), F32),
        pltpu.VMEM((mid + 1, 8, PAD), F32),
        pltpu.VMEM((Z, slots, half), F32),
        pltpu.VMEM((2, mid, slots, half), BF16),
        pltpu.VMEM((2, mid, slots, half), BF16),
        pltpu.VMEM((PAD, half), BF16),
        pltpu.VMEM((nb * rd, half), BF16),
        pltpu.VMEM((X, rd, width), BF16),
        pltpu.VMEM((nb * rd, half), BF16),
        dma((6,)),
    ]
    pairs = [(nb,), (2,), (nb, 2), (Z,), (mid + 1, nv), (mid + 1, nv), (2, mid, 2), (2, mid, 2), (2, mid, 2)]
    pairs += [(nb, 2), (nb, 2), (mid + 1, 2), (mid + 1, 2)]
    for shape in pairs:
        scratch += [dma(shape), dma(shape)]
    operands = (rows_in, expert_picks.T, latent_ids, enc_weight, dec_weight)
    return pl.pallas_call(
        functools.partial(step_kernel, X, Y, Z, slots, topk),
        out_shape=(
            pltpu.VMEM(rows_in.shape, BF16),
            pltpu.VMEM(enc_weight.shape, F32),
            pltpu.VMEM(dec_weight.shape, F32),
        ),
        in_specs=[hbm] * 5,
        out_specs=(vmem, vmem, vmem),
        scratch_shapes=scratch,
        compiler_params=pltpu.CompilerParams(
            collective_id=0, has_side_effects=True, vmem_limit_bytes=46 * 2**20
        ),
    )(*(pltpu.with_memory_space_constraint(a, pltpu.HBM) for a in operands))


def solution(mesh, experts=EXPERTS, topk=TOPK, cap=CAP):
    placed = (
        P("expert", "chan"),
        P("expert", None),
        P("expert", None, None),
        P("chan", "expert"),
        P("expert", "chan"),
    )
    return jax.shard_map(
        functools.partial(per_device, experts, topk, cap),
        mesh=mesh,
        in_specs=placed,
        out_specs=(P("expert", "chan"), P("chan", "expert"), P("expert", "chan")),
        check_vma=False,
    )
```

profile of v0, /device:TPU:1, one launch (start us, length us, event | category | flops | bytes accessed | tf_op | source)
XLA Modules:
  0.0 107.2 jit_solution(17153506783419617049)
XLA Ops:
  0.6 102.6 %shard_map.76 = (bf16[32,1536]{1,0:T(8,128)(2,1)S(1)}, f32[1536,512]{1,0:T(8,128)S(1)}, f32[512,1536]{1,0:T(8,128)S(1)}) custom-call(bf16[32,1536]{1,0:T(8,128)(2,1)} %rows_hbm.1, s32[2,32]{1,0:T(2,128)} %bitcast.1, s32[32,2,32]{2,1,0:T(2,128)} %ids_hbm.1, bf16[1536,512]{1,0:T(8,128)(2,1)} %enc_ref.1, bf16[512,1536]{1,0:T(8,128)(2,1)} %dec_ref.1), custom_call_target="tpu_custom_call" | custom-call | tf_op jit(solution)/shard_map/pallas_call | solution.py:567
  103.2 0.6 copy.11
  103.9 1.7 %copy.12 = f32[1536,512]{1,0:T(8,128)} copy(f32[1536,512]{1,0:T(8,128)S(1)} %get-tuple-element.4) | data formatting | bytes 6291456
  105.5 1.7 %copy.13 = f32[512,1536]{1,0:T(8,128)} copy(f32[512,1536]{1,0:T(8,128)S(1)} %get-tuple-element.5) | data formatting | bytes 6291456
where the time goes:
time: 107 us
  Pallas kernels  103 us (96%)
  local copies, waits for them, and re-layouts  3.97 us (4%)
    pallas_call x1, Pallas kernels, per_device(): pl.pallas_call(functools.partial(step_kernel, X, Y, Z, slots, topk), out_...  103 us
    unnamed x3, local copies, waits for them, and re-layouts  3.97 us

commit v1 on v0

--- a/solution.py
+++ b/solution.py
@@ -87,8 +87,8 @@
         buf[:, SLOTS:, :] = jnp.zeros((Z, PAD - SLOTS, half), BF16)
     fin[SLOTS:, :] = jnp.zeros((PAD - SLOTS, half), BF16)
     for s in range(mid + 1):
-        va[s, v] = jnp.zeros((8, PAD), F32)
-        vg[s, v] = jnp.zeros((8, PAD), F32)
+        va[v, s] = jnp.zeros((8, PAD), F32)
+        vg[v, s] = jnp.zeros((8, PAD), F32)
     genc_ref[...] = jnp.zeros_like(genc_ref)
     gdec_ref[...] = jnp.zeros_like(gdec_ref)
 
@@ -225,36 +225,45 @@
     def sides(s):
         return (0,) if isinstance(s, int) and s in (0, mid) else (0, 1)
 
-    def value_copy(buf, send, recv, s, i):
+    def run_of(buf, g):
+        if buf is va:
+            return (pl.ds(0, mid), pl.ds(mid, 1))[g]
+        return pl.ds(2 * g, 1 if isinstance(g, int) and 2 * g == mid else 2)
+
+    def value_copy(buf, send, recv, g, i):
         t = lax.rem(v + i, nv)
-        return remote(
-            buf.at[s, v], buf.at[s, v], send.at[s, i], recv.at[s, i], at(x, z, lax.rem(t, 2), t // 2)
-        )
-
-    def value_wait(buf, send, recv, s, i):
-        view = buf.at[s, lax.rem(v - i + nv, nv)]
-        remote(view, view, send.at[s, i], recv.at[s, i], twin).wait_recv()
+        view = buf.at[v, run_of(buf, g)]
+        return remote(view, view, send.at[g, i], recv.at[g, i], at(x, z, lax.rem(t, 2), t // 2))
+
+    def values_start(buf, send, recv, g):
+        for i in range(1, nv):
+            value_copy(buf, send, recv, g, i).start()
+
+    def values_wait(buf, send, recv, g):
+        for i in range(1, nv):
+            view = buf.at[lax.rem(v - i + nv, nv), run_of(buf, g)]
+            remote(view, view, send.at[g, i], recv.at[g, i], twin).wait_recv()
+
+    def values_left(buf, send, recv, g):
+        for i in range(1, nv):
+            value_copy(buf, send, recv, g, i).wait_send()
 
     def live_at(c, i):
         return lax.broadcasted_iota(jnp.int32, (STRIDE, PAD), 0) == offs[c, pl.ds(i, 1), :].astype(jnp.int32)
 
-    def partial_values(buf, send, recv, weight, chunks, s):
+    def partial_values(buf, weight, chunks, s):
         for j in sides(s):
             c = chunk_of(s, j)
             dense = nt(weight[...], chunks[c])
             for i in range(BLK):
-                buf[s, v, j * BLK + i : j * BLK + i + 1, :] = jnp.sum(
+                buf[v, s, j * BLK + i : j * BLK + i + 1, :] = jnp.sum(
                     jnp.where(live_at(c, i), dense[i * STRIDE : (i + 1) * STRIDE], 0.0), axis=0, keepdims=True
                 )
-        for i in range(1, nv):
-            value_copy(buf, send, recv, s, i).start()
-
-    def whole_values(buf, send, recv, s):
-        for i in range(1, nv):
-            value_wait(buf, send, recv, s, i)
-        total = buf[s, 0]
+
+    def whole_values(buf, s):
+        total = buf[0, s]
         for k in range(1, nv):
-            total += buf[s, k]
+            total += buf[k, s]
         return total
 
     def spread(values, c, i):
@@ -266,19 +275,17 @@
         rh[z, :, q * piece : (q + 1) * piece] = nn(pm[...], xbuf[:, q * piece : (q + 1) * piece]).astype(BF16)
         ring_begin(rh, a_send, a_recv, q, False)
 
-    def ro_copy(s, j):
-        return twin_copy(rh, ro, d_send, d_recv, s, j)
+    def ro_copy():
+        return remote(rh.at[:, pl.ds(0, SLOTS)], ro.at[:, pl.ds(0, SLOTS)], d_send.at[0], d_recv.at[0], twin)
 
     def eo_copy(s, j):
         return twin_copy(eh, eo, f_send, f_recv, s, j)
 
     def encode(s):
-        for j in sides(s):
-            ro_copy(s, j).start()
-        partial_values(va, va_send, va_recv, enct, rh, s)
+        partial_values(va, enct, rh, s)
 
     def decode(s):
-        values = whole_values(va, va_send, va_recv, s)
+        values = whole_values(va, s)
         vact[s] = values
         chunks = [chunk_of(s, j) for j in sides(s)]
         table = jnp.concatenate([values] + [offs[c] for c in chunks], axis=0).astype(BF16)
@@ -303,15 +310,6 @@
     encode(0)
     def encode_step(s, carry):
         ring_pass(rh, a_send, a_recv, s, 0, False)
-
-        @pl.when(s == 2)
-        def _():
-            decode(0)
-
-        @pl.when(s > 2)
-        def _():
-            decode(s - 2)
-
         ring_pass(rh, a_send, a_recv, s, 1, False)
 
         @pl.when(s == 1)
@@ -323,9 +321,12 @@
         return carry
 
     lax.fori_loop(1, mid, encode_step, 0)
-    decode(mid - 2)
+    values_start(va, va_send, va_recv, 0)
     ring_end(rh, a_send, a_recv)
     encode(mid)
+    values_start(va, va_send, va_recv, 1)
+    ro_copy().start()
+    values_wait(va, va_send, va_recv, 0)
     decode(mid - 1)
 
     def sum_copy(t, j, q):
@@ -335,15 +336,13 @@
             sbuf.at[j, t - 1, :, view], rbuf.at[j, t - 1, :, view], s_send.at[j, t - 1, q], s_recv.at[j, t - 1, q], to
         )
 
-    def transpose_rows(s):
+    def transpose_rows(k, src, s):
         for j in sides(s):
             c = chunk_of(s, j)
-            ro_copy(s, j).wait_recv()
-            for k, src in ((h, rh), (1 - h, ro)):
-                for i in range(half // 256):
-                    rowst[c, pl.ds(pl.multiple_of(k * half + i * 256, 256), 256), :] = nt(
-                        eye[...], src[c, :, i * 256 : (i + 1) * 256]
-                    ).astype(BF16)
+            for i in range(half // 256):
+                rowst[c, pl.ds(pl.multiple_of(k * half + i * 256, 256), 256), :] = nt(
+                    eye[...], src[c, :, i * 256 : (i + 1) * 256]
+                ).astype(BF16)
 
     def sum_step(t, k):
         for j in range(2):
@@ -358,17 +357,23 @@
             sum_copy(t, j, q).start()
 
     sum_step(mid - 1, 1)
+    decode(mid - 2)
+    values_wait(va, va_send, va_recv, 1)
     decode(mid)
     sum_step(mid, 0)
+    transpose_rows(h, rh, mid)
     sum_step(mid - 1, 0)
     pmt[...] = nt(eye[0:nr, 0:nr], pm[...]).astype(BF16)
-    transpose_rows(0)
+    transpose_rows(h, rh, 0)
     for t in range(mid - 2, 0, -1):
         sum_step(t, 1)
-        transpose_rows(t)
+        decode(t - 1)
+        transpose_rows(h, rh, t)
         sum_step(t, 0)
-    transpose_rows(mid - 1)
-    transpose_rows(mid)
+    transpose_rows(h, rh, mid - 1)
+    ro_copy().wait_recv()
+    for s in range(mid + 1):
+        transpose_rows(1 - h, ro, s)
 
     def ret_copy(i, q):
         t = lax.rem(b + i, nb)
@@ -423,7 +428,7 @@
     def latent_grads(s):
         for j in sides(s):
             eo_copy(s, j).start()
-        partial_values(vg, vg_send, vg_recv, dech, eh, s)
+        partial_values(vg, dech, eh, s)
 
     def add_dec(s):
         for j in sides(s):
@@ -438,7 +443,7 @@
             gdec_ref[:, lanes(k)] += sum(nn(a, src[c]) for c, a in acts)
 
     def add_enc(s):
-        vpre[s] = whole_values(vg, vg_send, vg_recv, s)
+        vpre[s] = whole_values(vg, s)
         for i in range(lat // STRIDE):
             blk = h * (lat // STRIDE) + i
             low = i * STRIDE
@@ -458,14 +463,19 @@
 
         @pl.when(s == 2)
         def _():
+            values_wait(vg, vg_send, vg_recv, 0)
             add_enc(0)
 
-        @pl.when(s > 2)
+        @pl.when(s == 3)
         def _():
-            add_enc(s - 2)
+            add_enc(1)
 
         ring_pass(eh, b_send, b_recv, s, 1, False)
         latent_grads(s)
+
+        @pl.when(lax.rem(s, 2) == 1)
+        def _():
+            values_start(vg, vg_send, vg_recv, s // 2)
 
         @pl.when(s > 1)
         def _():
@@ -474,12 +484,15 @@
         return carry
 
     lax.fori_loop(1, mid, gradient_step, 0)
-    add_enc(mid - 2)
     ring_end(eh, b_send, b_recv)
     latent_grads(mid)
+    values_start(vg, vg_send, vg_recv, mid // 2)
     add_dec(mid - 1)
+    values_wait(vg, vg_send, vg_recv, mid // 2 - 1)
+    add_enc(mid - 2)
     add_enc(mid - 1)
     add_dec(mid)
+    values_wait(vg, vg_send, vg_recv, mid // 2)
     add_enc(mid)
 
     for i in range(1, nb):
@@ -500,21 +513,37 @@
                 if t < mid or q == j:
                     sum_copy(t, j, q).wait_send()
 
-    def sent(s):
-        for i in range(1, nv):
-            value_copy(va, va_send, va_recv, s, i).wait_send()
-            value_copy(vg, vg_send, vg_recv, s, i).wait_send()
+    for g in range(2):
+        values_left(va, va_send, va_recv, g)
+    for g in range(mid // 2 + 1):
+        values_left(vg, vg_send, vg_recv, g)
+    ro_copy().wait_send()
+
+    def eo_left(s):
         for j in sides(s):
-            ro_copy(s, j).wait_send()
             eo_copy(s, j).wait_send()
 
-    def sent_step(s, carry):
-        sent(s)
+    def eo_left_step(s, carry):
+        eo_left(s)
         return carry
 
-    sent(0)
-    lax.fori_loop(1, mid, sent_step, 0)
-    sent(mid)
+    eo_left(0)
+    lax.fori_loop(1, mid, eo_left_step, 0)
+    eo_left(mid)
+
+
+def write_out(*refs):
+    srcs, dsts, sems = refs[:3], refs[3:6], refs[6]
+    copies = []
+    for src, dst, parts in zip(srcs, dsts, (1, 4, 4)):
+        n = src.shape[0] // parts
+        for k in range(parts):
+            rows = pl.ds(k * n, n)
+            copies.append(pltpu.make_async_copy(src.at[rows], dst.at[rows], sems.at[len(copies)]))
+    for c in copies:
+        c.start()
+    for c in copies:
+        c.wait()
 
 
 def per_device(experts, topk, cap, rows_in, expert_picks, latent_ids, enc_weight, dec_weight):
@@ -546,8 +575,8 @@
         pltpu.VMEM((nb * rd, PAD), BF16),
         pltpu.VMEM((Z, 8, PAD), F32),
         pltpu.VMEM((Z, 8, PAD), F32),
-        pltpu.VMEM((mid + 1, nv, 8, PAD), F32),
-        pltpu.VMEM((mid + 1, nv, 8, PAD), F32),
+        pltpu.VMEM((nv, mid + 1, 8, PAD), F32),
+        pltpu.VMEM((nv, mid + 1, 8, PAD), F32),
         pltpu.VMEM((mid + 1, 8, PAD), F32),
         pltpu.VMEM((mid + 1, 8, PAD), F32),
         pltpu.VMEM((Z, slots, half), F32),
@@ -559,12 +588,12 @@
         pltpu.VMEM((nb * rd, half), BF16),
         dma((6,)),
     ]
-    pairs = [(nb,), (2,), (nb, 2), (Z,), (mid + 1, nv), (mid + 1, nv), (2, mid, 2), (2, mid, 2), (2, mid, 2)]
-    pairs += [(nb, 2), (nb, 2), (mid + 1, 2), (mid + 1, 2)]
+    pairs = [(nb,), (2,), (nb, 2), (Z,), (2, nv), (mid // 2 + 1, nv), (2, mid, 2), (2, mid, 2), (2, mid, 2)]
+    pairs += [(nb, 2), (nb, 2), (1,), (mid + 1, 2)]
     for shape in pairs:
         scratch += [dma(shape), dma(shape)]
     operands = (rows_in, expert_picks.T, latent_ids, enc_weight, dec_weight)
-    return pl.pallas_call(
+    results = pl.pallas_call(
         functools.partial(step_kernel, X, Y, Z, slots, topk),
         out_shape=(
             pltpu.VMEM(rows_in.shape, BF16),
@@ -578,6 +607,14 @@
             collective_id=0, has_side_effects=True, vmem_limit_bytes=46 * 2**20
         ),
     )(*(pltpu.with_memory_space_constraint(a, pltpu.HBM) for a in operands))
+    return pl.pallas_call(
+        write_out,
+        out_shape=tuple(jax.ShapeDtypeStruct(r.shape, r.dtype) for r in results),
+        in_specs=[vmem] * 3,
+        out_specs=(hbm,) * 3,
+        scratch_shapes=[dma((9,))],
+        compiler_params=pltpu.CompilerParams(vmem_limit_bytes=2 * 2**20),
+    )(*(pltpu.with_memory_space_constraint(r, pltpu.VMEM) for r in results))
 
 
 def solution(mesh, experts=EXPERTS, topk=TOPK, cap=CAP):

time: 107 us -> 106 us (level)
  local copies, waits for them, and re-layouts: 3.97 us -> 0 us
  Pallas kernels: 103 us -> 105 us
    unnamed x3 -> x0, local copies, waits for them, and re-layouts: 3.97 us -> none
    pallas_call x0 -> x1, Pallas kernels: none -> 2.78 us  [per_device(): pl.pallas_call(write_out, out_shape=tuple((jax.ShapeDtypeStruct(r.shape,...]
where the time goes in v1:
time: 106 us
  Pallas kernels  105 us (99%)
    pallas_call x1, Pallas kernels, per_device(): pl.pallas_call(functools.partial(step_kernel, X, Y, Z, slots, topk), out_...  103 us
    pallas_call x1, Pallas kernels, per_device(): pl.pallas_call(write_out, out_shape=tuple((jax.ShapeDtypeStruct(r.shape,...  2.78 us

profile of v1, /device:TPU:1, one launch (start us, length us, event | category | flops | bytes accessed | tf_op | source)
XLA Modules:
  0.0 106.1 jit_solution(12697654232867333224)
XLA Ops:
  0.6 102.5 %shard_map.76 = (bf16[32,1536]{1,0:T(8,128)(2,1)S(1)}, f32[1536,512]{1,0:T(8,128)S(1)}, f32[512,1536]{1,0:T(8,128)S(1)}) custom-call(bf16[32,1536]{1,0:T(8,128)(2,1)} %rows_hbm.1, s32[2,32]{1,0:T(2,128)} %bitcast.1, s32[32,2,32]{2,1,0:T(2,128)} %ids_hbm.1, bf16[1536,512]{1,0:T(8,128)(2,1)} %enc_ref.1, bf16[512,1536]{1,0:T(8,128)(2,1)} %dec_ref.1), custom_call_target="tpu_custom_call" | custom-call | tf_op jit(solution)/shard_map/pallas_call | solution.py:596
  103.2 2.8 %shard_map.77 = (bf16[32,1536]{1,0:T(8,128)(2,1)}, f32[1536,512]{1,0:T(8,128)}, f32[512,1536]{1,0:T(8,128)}) custom-call(bf16[32,1536]{1,0:T(8,128)(2,1)S(1)} %get-tuple-element.6.refs_0_, f32[1536,512]{1,0:T(8,128)S(1)} %get-tuple-element.7.refs_1_, f32[512,1536]{1,0:T(8,128)S(1)} %get-tuple-element.8.refs_2_), custom_call_target="tpu_custom_call" | custom-call | tf_op jit(solution)/shard_map/pallas_call | solution.py:610
